TPU v7x, 512 devices: a whole 4x4x16 slice. The times are simulated.
512 devices in a mesh: section: 16 (over z), expert: 32 (over y, x, core).
Axes of the slice: x: 4, y: 4, z: 16, core: 2. Of those that a mesh axis runs over, the one named last changes fastest.
Arguments:
- tokens: bfloat16 [8, 256, 2048], P(None, 'expert', 'section'), may hold values from -6 to 6
- norm_gain: float32 [16, 2048], P('section'), may hold values from 0.1 to 1.9
- gate_weight: bfloat16 [16, 32, 2048, 384], P('section', 'expert'), may hold values from -0.125 to 0.125
- up_weight: bfloat16 [16, 32, 2048, 384], P('section', 'expert'), may hold values from -0.125 to 0.125
- down_weight: bfloat16 [16, 32, 384, 2048], P('section', 'expert'), may hold values from -0.3125 to 0.3125
- expert_ids: int32 [16, 8, 256, 8], P('section', None, 'expert'), may hold values from 0 to 31, all different within a row; in each aligned block of 8 rows (0 to 7, 8 to 15, ..., all dimensions but the last counted through in order) at most 2 rows name the same one
- gate_probs: float32 [16, 8, 256, 8], P('section', None, 'expert'), may hold values from 0.05 to 1
Outputs:
- hidden_states: bfloat16 [16, 8, 256, 2048], P('section', None, 'expert')
Inputs may be any that keep to these rules, and one draw needn't show every extreme that they name: `expert_ids`: in the 8 rows of one index of expert for one layer and micro-batch (aligned blocks of 8 rows), no expert is named by more than 2 rows, a bound that some block reaches in every draw.
All inputs are finite; a program needn't handle non-finite values.
Results may differ from a plain program's by a relative error of at most 0.04.
Values may be sent and summed in bfloat16 or wider, within the bound.
No kernel may reach another device: no remote copies, remote signals or barrier semaphores. Data moves between devices by JAX's collectives and lax.ppermute only.
A program may use at most 64 MiB of HBM per device.

v0:
```python
import jax
import jax.numpy as jnp
from jax import lax
from jax.sharding import PartitionSpec as P

CAP = 2
EPS = 1e-06


def passed_along(value, axis, by):
    length = lax.axis_size(axis)
    pairs = [(i, i + by) for i in range(length) if 0 <= i + by < length]
    return lax.ppermute(value, axis, pairs)


def expert_block(routed, w_gate, w_up, w_down):
    gate_proj = jnp.einsum("escd,edf->escf", routed, w_gate, preferred_element_type=jnp.float32)
    up_proj = jnp.einsum("escd,edf->escf", routed, w_up, preferred_element_type=jnp.float32)
    active = (jax.nn.silu(gate_proj) * up_proj).astype(jnp.bfloat16)
    return jnp.einsum("escf,efd->escd", active, w_down, preferred_element_type=jnp.float32).astype(
        jnp.bfloat16
    )


def slot_numbers(flat_ids, experts, capacity):
    onehot = (flat_ids[..., None] == jnp.arange(experts, dtype=jnp.int32)).astype(jnp.int32)
    before = jnp.cumsum(onehot, axis=-2) - onehot
    return flat_ids * capacity + jnp.sum(onehot * before, axis=-1)


def moe_layer(layer_input, norm_scale, expert_list, gate_share, w_gate, w_up, w_down):
    row_count, columns = layer_input.shape
    top_count = expert_list.shape[1]
    experts_local = w_gate.shape[0]
    groups = lax.axis_size("expert")
    experts = experts_local * groups
    capacity = CAP
    widened = layer_input.astype(jnp.float32)
    normed = (
        widened * lax.rsqrt(jnp.mean(widened * widened, axis=-1, keepdims=True) + EPS) * norm_scale
    ).astype(jnp.bfloat16)
    weight = gate_share / jnp.sum(gate_share, axis=-1, keepdims=True)
    slot_index = slot_numbers(
        expert_list.reshape(row_count * top_count), experts, capacity
    ).reshape(row_count, top_count)
    target = jnp.arange(experts * capacity, dtype=jnp.int32)
    placement = jnp.sum(
        (slot_index[None, :, :] == target[:, None, None]).astype(jnp.bfloat16), axis=2
    )
    sending = jnp.dot(placement, normed, preferred_element_type=jnp.float32).astype(jnp.bfloat16)
    sending = sending.reshape(experts, 1, capacity, columns)
    results = expert_block(
        lax.all_to_all(sending, "expert", split_axis=0, concat_axis=1, tiled=True),
        w_gate,
        w_up,
        w_down,
    )
    returned = lax.all_to_all(results, "expert", split_axis=1, concat_axis=0, tiled=True)
    returns_wide = returned.reshape(experts * capacity, columns).astype(jnp.float32)
    mixing = jnp.sum(
        (slot_index[:, :, None] == target[None, None, :]).astype(jnp.float32) * weight[:, :, None],
        axis=1,
    )
    mixed = jnp.dot(mixing, returns_wide, precision=lax.Precision.HIGHEST)
    return (widened + mixed).astype(jnp.bfloat16)


def local(tokens, norm_gain, gate_weight, up_weight, down_weight, expert_ids, gate_probs):
    section_index = lax.axis_index("section")
    section_count = lax.axis_size("section")
    full_tokens = lax.all_gather(tokens, "section", axis=2, tiled=True)
    micro_count, row_count, columns = full_tokens.shape
    turn_count = section_count + micro_count - 1
    norm_scale = norm_gain[0]
    w_gate = gate_weight[0]
    w_up = up_weight[0]
    w_down = down_weight[0]
    layer_ids = expert_ids[0]
    layer_probs = gate_probs[0]

    def advance(turn_index, state_pair):
        incoming, hidden_out = state_pair
        micro_index = turn_index - section_index
        is_valid = (micro_index >= 0) & (micro_index < micro_count)
        micro_pick = jnp.clip(micro_index, 0, micro_count - 1)
        fresh_rows = lax.dynamic_index_in_dim(full_tokens, micro_pick, 0, keepdims=False)
        layer_input = jnp.where(section_index == 0, fresh_rows, incoming)
        expert_list = lax.dynamic_index_in_dim(layer_ids, micro_pick, 0, keepdims=False)
        gate_share = lax.dynamic_index_in_dim(layer_probs, micro_pick, 0, keepdims=False)
        layer_output = moe_layer(
            layer_input, norm_scale, expert_list, gate_share, w_gate, w_up, w_down
        )
        updated = lax.dynamic_update_index_in_dim(hidden_out, layer_output, micro_pick, 0)
        hidden_out = jnp.where(is_valid, updated, hidden_out)
        passed = passed_along(layer_output, "section", 1)
        return (passed, hidden_out)

    initial = (
        jnp.zeros((row_count, columns), jnp.bfloat16),
        jnp.zeros((micro_count, row_count, columns), jnp.bfloat16),
    )
    final_pair = lax.fori_loop(0, turn_count, advance, initial)
    return final_pair[1][None]


def solution(mesh):
    in_specs = (
        P(None, "expert", "section"),
        P("section", None),
        P("section", "expert", None, None),
        P("section", "expert", None, None),
        P("section", "expert", None, None),
        P("section", None, "expert", None),
        P("section", None, "expert", None),
    )
    out_specs = P("section", None, "expert", None)
    return jax.shard_map(local, mesh=mesh, in_specs=in_specs, out_specs=out_specs, check_vma=False)
```

profile of v0, /device:TPU:128, one launch (start us, length us, event | category | flops | bytes accessed | tf_op | source)
XLA Modules:
  0.0 1059.5 jit_solution(3199038238281607523)
XLA Ops:
  0.0 33.5 %all_gather.3 = bf16[8,8,2048]{2,1,0:T(8,128)(2,1)} all-gather(bf16[8,8,128]{2,1,0:T(8,128)(2,1)} %param.9), channel_id=1, replica_groups=mesh['section'=16,'expert'=32] {'section'}, dimensions={2}, use_global_device_ids=true | all-gather | bytes 278528 | tf_op jit(solution)/shard_map/all_gather | solution.py:71
  34.2 1025.2 %while.17 = (s32[]{:T(128)}, bf16[8,2048]{1,0:T(8,128)(2,1)S(1)}, bf16[8,8,2048]{2,1,0:T(8,128)(2,1)}, pred[]{:T(512)}, s32[]{:T(128)}, /*index=5*/bf16[8,8,2048...) while((s32[]{:T(128)}, bf16[8,2048]{1,0:T(8,128)(2,1)S(1)}, ...), condition=%wide.region_7.8_spmd, body=%wide.region_0.7_spmd.sunk | while | flops 317443392 | bytes 22401360 | solution.py:102
  39.1 7.3 all-to-all-start
  48.0 7.3 all-to-all-done
  65.3 8.0 all-to-all-done.1
  92.5 7.3 all-to-all-done
  109.8 8.0 all-to-all-done.1
  136.9 7.3 all-to-all-done
  154.2 8.0 all-to-all-done.1
  181.3 7.3 all-to-all-done
  198.6 8.0 all-to-all-done.1
  225.7 7.3 all-to-all-done
  243.0 8.0 all-to-all-done.1
  270.2 7.3 all-to-all-done
  287.5 8.0 all-to-all-done.1
  314.6 7.3 all-to-all-done
  331.9 8.0 all-to-all-done.1
  359.0 7.3 all-to-all-done
  376.3 8.0 all-to-all-done.1
  403.4 7.3 all-to-all-done
  420.7 8.0 all-to-all-done.1
  447.9 7.3 all-to-all-done
  465.2 8.0 all-to-all-done.1
  492.3 7.3 all-to-all-done
  509.6 8.0 all-to-all-done.1
  536.7 7.3 all-to-all-done
  554.0 8.0 all-to-all-done.1
  581.1 7.3 all-to-all-done
  598.4 8.0 all-to-all-done.1
  625.6 7.3 all-to-all-done
  642.9 8.0 all-to-all-done.1
  670.0 7.3 all-to-all-done
  687.3 8.0 all-to-all-done.1
  714.4 7.3 all-to-all-done
  731.7 8.0 all-to-all-done.1
  758.9 7.3 all-to-all-done
  776.1 8.0 all-to-all-done.1
  803.3 7.3 all-to-all-done
  820.6 8.0 all-to-all-done.1
  847.7 7.3 all-to-all-done
  865.0 8.0 all-to-all-done.1
  892.1 7.3 all-to-all-done
  909.4 8.0 all-to-all-done.1
  936.6 7.3 all-to-all-done
  953.9 8.0 all-to-all-done.1
  981.0 7.3 all-to-all-done
  998.3 8.0 all-to-all-done.1
  1042.7 8.0 all-to-all-done.1
  (692 shorter events, 670.6 us)
Async XLA Ops:
  39.1 16.2 %all-to-all-start = ((bf16[32,1,2,2048]{3,2,1,0:T(2,128)(2,1)}), bf16[32,1,2,2048]{3,2,1,0:T(2,128)(2,1)S(1)}, u32[]{:S(2)}, u32[]{:S(2)}) async-start(bf16[32,1,2,2048]{3,2,1,0:T(2,128)(2,1)} %bitcast.85), calls=%async_computation | async-start | bytes 524288 | tf_op jit(solution)/shard_map/while/body/eval_jaxpr/all_to_all | solution.py:53
  60.6 12.8 %all-to-all-start.1 = ((bf16[1,32,2,2048]{3,2,0,1:T(2,128)(2,1)}), bf16[1,32,2,2048]{3,2,0,1:T(2,128)(2,1)S(1)}, u32[]{:S(2)}, u32[]{:S(2)}) async-start(bf16[1,32,2,2048]{3,2,0,1:T(2,128)(2,1)} %copy.31), calls=%async_computation.1 | async-start | bytes 524288 | tf_op jit(solution)/shard_map/while/body/eval_jaxpr/all_to_all | solution.py:58
  87.0 12.8 %all-to-all-start = ((bf16[32,1,2,2048]{3,2,1,0:T(2,128)(2,1)}), bf16[32,1,2,2048]{3,2,1,0:T(2,128)(2,1)S(1)}, u32[]{:S(2)}, u32[]{:S(2)}) async-start(bf16[32,1,2,2048]{3,2,1,0:T(2,128)(2,1)} %bitcast.85), calls=%async_computation | async-start | bytes 524288 | tf_op jit(solution)/shard_map/while/body/eval_jaxpr/all_to_all | solution.py:53
  105.0 12.8 %all-to-all-start.1 = ((bf16[1,32,2,2048]{3,2,0,1:T(2,128)(2,1)}), bf16[1,32,2,2048]{3,2,0,1:T(2,128)(2,1)S(1)}, u32[]{:S(2)}, u32[]{:S(2)}) async-start(bf16[1,32,2,2048]{3,2,0,1:T(2,128)(2,1)} %copy.31), calls=%async_computation.1 | async-start | bytes 524288 | tf_op jit(solution)/shard_map/while/body/eval_jaxpr/all_to_all | solution.py:58
  131.4 12.8 %all-to-all-start = ((bf16[32,1,2,2048]{3,2,1,0:T(2,128)(2,1)}), bf16[32,1,2,2048]{3,2,1,0:T(2,128)(2,1)S(1)}, u32[]{:S(2)}, u32[]{:S(2)}) async-start(bf16[32,1,2,2048]{3,2,1,0:T(2,128)(2,1)} %bitcast.85), calls=%async_computation | async-start | bytes 524288 | tf_op jit(solution)/shard_map/while/body/eval_jaxpr/all_to_all | solution.py:53
  149.5 12.8 %all-to-all-start.1 = ((bf16[1,32,2,2048]{3,2,0,1:T(2,128)(2,1)}), bf16[1,32,2,2048]{3,2,0,1:T(2,128)(2,1)S(1)}, u32[]{:S(2)}, u32[]{:S(2)}) async-start(bf16[1,32,2,2048]{3,2,0,1:T(2,128)(2,1)} %copy.31), calls=%async_computation.1 | async-start | bytes 524288 | tf_op jit(solution)/shard_map/while/body/eval_jaxpr/all_to_all | solution.py:58
  175.9 12.8 %all-to-all-start = ((bf16[32,1,2,2048]{3,2,1,0:T(2,128)(2,1)}), bf16[32,1,2,2048]{3,2,1,0:T(2,128)(2,1)S(1)}, u32[]{:S(2)}, u32[]{:S(2)}) async-start(bf16[32,1,2,2048]{3,2,1,0:T(2,128)(2,1)} %bitcast.85), calls=%async_computation | async-start | bytes 524288 | tf_op jit(solution)/shard_map/while/body/eval_jaxpr/all_to_all | solution.py:53
  193.9 12.8 %all-to-all-start.1 = ((bf16[1,32,2,2048]{3,2,0,1:T(2,128)(2,1)}), bf16[1,32,2,2048]{3,2,0,1:T(2,128)(2,1)S(1)}, u32[]{:S(2)}, u32[]{:S(2)}) async-start(bf16[1,32,2,2048]{3,2,0,1:T(2,128)(2,1)} %copy.31), calls=%async_computation.1 | async-start | bytes 524288 | tf_op jit(solution)/shard_map/while/body/eval_jaxpr/all_to_all | solution.py:58
  220.3 12.8 %all-to-all-start = ((bf16[32,1,2,2048]{3,2,1,0:T(2,128)(2,1)}), bf16[32,1,2,2048]{3,2,1,0:T(2,128)(2,1)S(1)}, u32[]{:S(2)}, u32[]{:S(2)}) async-start(bf16[32,1,2,2048]{3,2,1,0:T(2,128)(2,1)} %bitcast.85), calls=%async_computation | async-start | bytes 524288 | tf_op jit(solution)/shard_map/while/body/eval_jaxpr/all_to_all | solution.py:53
  238.3 12.8 %all-to-all-start.1 = ((bf16[1,32,2,2048]{3,2,0,1:T(2,128)(2,1)}), bf16[1,32,2,2048]{3,2,0,1:T(2,128)(2,1)S(1)}, u32[]{:S(2)}, u32[]{:S(2)}) async-start(bf16[1,32,2,2048]{3,2,0,1:T(2,128)(2,1)} %copy.31), calls=%async_computation.1 | async-start | bytes 524288 | tf_op jit(solution)/shard_map/while/body/eval_jaxpr/all_to_all | solution.py:58
  252.8 7.0 collective-permute-start
  264.7 12.8 %all-to-all-start = ((bf16[32,1,2,2048]{3,2,1,0:T(2,128)(2,1)}), bf16[32,1,2,2048]{3,2,1,0:T(2,128)(2,1)S(1)}, u32[]{:S(2)}, u32[]{:S(2)}) async-start(bf16[32,1,2,2048]{3,2,1,0:T(2,128)(2,1)} %bitcast.85), calls=%async_computation | async-start | bytes 524288 | tf_op jit(solution)/shard_map/while/body/eval_jaxpr/all_to_all | solution.py:53
  282.7 12.8 %all-to-all-start.1 = ((bf16[1,32,2,2048]{3,2,0,1:T(2,128)(2,1)}), bf16[1,32,2,2048]{3,2,0,1:T(2,128)(2,1)S(1)}, u32[]{:S(2)}, u32[]{:S(2)}) async-start(bf16[1,32,2,2048]{3,2,0,1:T(2,128)(2,1)} %copy.31), calls=%async_computation.1 | async-start | bytes 524288 | tf_op jit(solution)/shard_map/while/body/eval_jaxpr/all_to_all | solution.py:58
  309.1 12.8 %all-to-all-start = ((bf16[32,1,2,2048]{3,2,1,0:T(2,128)(2,1)}), bf16[32,1,2,2048]{3,2,1,0:T(2,128)(2,1)S(1)}, u32[]{:S(2)}, u32[]{:S(2)}) async-start(bf16[32,1,2,2048]{3,2,1,0:T(2,128)(2,1)} %bitcast.85), calls=%async_computation | async-start | bytes 524288 | tf_op jit(solution)/shard_map/while/body/eval_jaxpr/all_to_all | solution.py:53
  327.2 12.8 %all-to-all-start.1 = ((bf16[1,32,2,2048]{3,2,0,1:T(2,128)(2,1)}), bf16[1,32,2,2048]{3,2,0,1:T(2,128)(2,1)S(1)}, u32[]{:S(2)}, u32[]{:S(2)}) async-start(bf16[1,32,2,2048]{3,2,0,1:T(2,128)(2,1)} %copy.31), calls=%async_computation.1 | async-start | bytes 524288 | tf_op jit(solution)/shard_map/while/body/eval_jaxpr/all_to_all | solution.py:58
  353.6 12.8 %all-to-all-start = ((bf16[32,1,2,2048]{3,2,1,0:T(2,128)(2,1)}), bf16[32,1,2,2048]{3,2,1,0:T(2,128)(2,1)S(1)}, u32[]{:S(2)}, u32[]{:S(2)}) async-start(bf16[32,1,2,2048]{3,2,1,0:T(2,128)(2,1)} %bitcast.85), calls=%async_computation | async-start | bytes 524288 | tf_op jit(solution)/shard_map/while/body/eval_jaxpr/all_to_all | solution.py:53
  371.6 12.8 %all-to-all-start.1 = ((bf16[1,32,2,2048]{3,2,0,1:T(2,128)(2,1)}), bf16[1,32,2,2048]{3,2,0,1:T(2,128)(2,1)S(1)}, u32[]{:S(2)}, u32[]{:S(2)}) async-start(bf16[1,32,2,2048]{3,2,0,1:T(2,128)(2,1)} %copy.31), calls=%async_computation.1 | async-start | bytes 524288 | tf_op jit(solution)/shard_map/while/body/eval_jaxpr/all_to_all | solution.py:58
  398.0 12.8 %all-to-all-start = ((bf16[32,1,2,2048]{3,2,1,0:T(2,128)(2,1)}), bf16[32,1,2,2048]{3,2,1,0:T(2,128)(2,1)S(1)}, u32[]{:S(2)}, u32[]{:S(2)}) async-start(bf16[32,1,2,2048]{3,2,1,0:T(2,128)(2,1)} %bitcast.85), calls=%async_computation | async-start | bytes 524288 | tf_op jit(solution)/shard_map/while/body/eval_jaxpr/all_to_all | solution.py:53
  416.0 12.8 %all-to-all-start.1 = ((bf16[1,32,2,2048]{3,2,0,1:T(2,128)(2,1)}), bf16[1,32,2,2048]{3,2,0,1:T(2,128)(2,1)S(1)}, u32[]{:S(2)}, u32[]{:S(2)}) async-start(bf16[1,32,2,2048]{3,2,0,1:T(2,128)(2,1)} %copy.31), calls=%async_computation.1 | async-start | bytes 524288 | tf_op jit(solution)/shard_map/while/body/eval_jaxpr/all_to_all | solution.py:58
  442.4 12.8 %all-to-all-start = ((bf16[32,1,2,2048]{3,2,1,0:T(2,128)(2,1)}), bf16[32,1,2,2048]{3,2,1,0:T(2,128)(2,1)S(1)}, u32[]{:S(2)}, u32[]{:S(2)}) async-start(bf16[32,1,2,2048]{3,2,1,0:T(2,128)(2,1)} %bitcast.85), calls=%async_computation | async-start | bytes 524288 | tf_op jit(solution)/shard_map/while/body/eval_jaxpr/all_to_all | solution.py:53
  460.4 12.8 %all-to-all-start.1 = ((bf16[1,32,2,2048]{3,2,0,1:T(2,128)(2,1)}), bf16[1,32,2,2048]{3,2,0,1:T(2,128)(2,1)S(1)}, u32[]{:S(2)}, u32[]{:S(2)}) async-start(bf16[1,32,2,2048]{3,2,0,1:T(2,128)(2,1)} %copy.31), calls=%async_computation.1 | async-start | bytes 524288 | tf_op jit(solution)/shard_map/while/body/eval_jaxpr/all_to_all | solution.py:58
  486.8 12.8 %all-to-all-start = ((bf16[32,1,2,2048]{3,2,1,0:T(2,128)(2,1)}), bf16[32,1,2,2048]{3,2,1,0:T(2,128)(2,1)S(1)}, u32[]{:S(2)}, u32[]{:S(2)}) async-start(bf16[32,1,2,2048]{3,2,1,0:T(2,128)(2,1)} %bitcast.85), calls=%async_computation | async-start | bytes 524288 | tf_op jit(solution)/shard_map/while/body/eval_jaxpr/all_to_all | solution.py:53
  504.9 12.8 %all-to-all-start.1 = ((bf16[1,32,2,2048]{3,2,0,1:T(2,128)(2,1)}), bf16[1,32,2,2048]{3,2,0,1:T(2,128)(2,1)S(1)}, u32[]{:S(2)}, u32[]{:S(2)}) async-start(bf16[1,32,2,2048]{3,2,0,1:T(2,128)(2,1)} %copy.31), calls=%async_computation.1 | async-start | bytes 524288 | tf_op jit(solution)/shard_map/while/body/eval_jaxpr/all_to_all | solution.py:58
  531.3 12.8 %all-to-all-start = ((bf16[32,1,2,2048]{3,2,1,0:T(2,128)(2,1)}), bf16[32,1,2,2048]{3,2,1,0:T(2,128)(2,1)S(1)}, u32[]{:S(2)}, u32[]{:S(2)}) async-start(bf16[32,1,2,2048]{3,2,1,0:T(2,128)(2,1)} %bitcast.85), calls=%async_computation | async-start | bytes 524288 | tf_op jit(solution)/shard_map/while/body/eval_jaxpr/all_to_all | solution.py:53
  549.3 12.8 %all-to-all-start.1 = ((bf16[1,32,2,2048]{3,2,0,1:T(2,128)(2,1)}), bf16[1,32,2,2048]{3,2,0,1:T(2,128)(2,1)S(1)}, u32[]{:S(2)}, u32[]{:S(2)}) async-start(bf16[1,32,2,2048]{3,2,0,1:T(2,128)(2,1)} %copy.31), calls=%async_computation.1 | async-start | bytes 524288 | tf_op jit(solution)/shard_map/while/body/eval_jaxpr/all_to_all | solution.py:58
  563.8 7.0 collective-permute-start
  575.7 12.8 %all-to-all-start = ((bf16[32,1,2,2048]{3,2,1,0:T(2,128)(2,1)}), bf16[32,1,2,2048]{3,2,1,0:T(2,128)(2,1)S(1)}, u32[]{:S(2)}, u32[]{:S(2)}) async-start(bf16[32,1,2,2048]{3,2,1,0:T(2,128)(2,1)} %bitcast.85), calls=%async_computation | async-start | bytes 524288 | tf_op jit(solution)/shard_map/while/body/eval_jaxpr/all_to_all | solution.py:53
  593.7 12.8 %all-to-all-start.1 = ((bf16[1,32,2,2048]{3,2,0,1:T(2,128)(2,1)}), bf16[1,32,2,2048]{3,2,0,1:T(2,128)(2,1)S(1)}, u32[]{:S(2)}, u32[]{:S(2)}) async-start(bf16[1,32,2,2048]{3,2,0,1:T(2,128)(2,1)} %copy.31), calls=%async_computation.1 | async-start | bytes 524288 | tf_op jit(solution)/shard_map/while/body/eval_jaxpr/all_to_all | solution.py:58
  620.1 12.8 %all-to-all-start = ((bf16[32,1,2,2048]{3,2,1,0:T(2,128)(2,1)}), bf16[32,1,2,2048]{3,2,1,0:T(2,128)(2,1)S(1)}, u32[]{:S(2)}, u32[]{:S(2)}) async-start(bf16[32,1,2,2048]{3,2,1,0:T(2,128)(2,1)} %bitcast.85), calls=%async_computation | async-start | bytes 524288 | tf_op jit(solution)/shard_map/while/body/eval_jaxpr/all_to_all | solution.py:53
  638.1 12.8 %all-to-all-start.1 = ((bf16[1,32,2,2048]{3,2,0,1:T(2,128)(2,1)}), bf16[1,32,2,2048]{3,2,0,1:T(2,128)(2,1)S(1)}, u32[]{:S(2)}, u32[]{:S(2)}) async-start(bf16[1,32,2,2048]{3,2,0,1:T(2,128)(2,1)} %copy.31), calls=%async_computation.1 | async-start | bytes 524288 | tf_op jit(solution)/shard_map/while/body/eval_jaxpr/all_to_all | solution.py:58
  664.5 12.8 %all-to-all-start = ((bf16[32,1,2,2048]{3,2,1,0:T(2,128)(2,1)}), bf16[32,1,2,2048]{3,2,1,0:T(2,128)(2,1)S(1)}, u32[]{:S(2)}, u32[]{:S(2)}) async-start(bf16[32,1,2,2048]{3,2,1,0:T(2,128)(2,1)} %bitcast.85), calls=%async_computation | async-start | bytes 524288 | tf_op jit(solution)/shard_map/while/body/eval_jaxpr/all_to_all | solution.py:53
  682.6 12.8 %all-to-all-start.1 = ((bf16[1,32,2,2048]{3,2,0,1:T(2,128)(2,1)}), bf16[1,32,2,2048]{3,2,0,1:T(2,128)(2,1)S(1)}, u32[]{:S(2)}, u32[]{:S(2)}) async-start(bf16[1,32,2,2048]{3,2,0,1:T(2,128)(2,1)} %copy.31), calls=%async_computation.1 | async-start | bytes 524288 | tf_op jit(solution)/shard_map/while/body/eval_jaxpr/all_to_all | solution.py:58
  709.0 12.8 %all-to-all-start = ((bf16[32,1,2,2048]{3,2,1,0:T(2,128)(2,1)}), bf16[32,1,2,2048]{3,2,1,0:T(2,128)(2,1)S(1)}, u32[]{:S(2)}, u32[]{:S(2)}) async-start(bf16[32,1,2,2048]{3,2,1,0:T(2,128)(2,1)} %bitcast.85), calls=%async_computation | async-start | bytes 524288 | tf_op jit(solution)/shard_map/while/body/eval_jaxpr/all_to_all | solution.py:53
  727.0 12.8 %all-to-all-start.1 = ((bf16[1,32,2,2048]{3,2,0,1:T(2,128)(2,1)}), bf16[1,32,2,2048]{3,2,0,1:T(2,128)(2,1)S(1)}, u32[]{:S(2)}, u32[]{:S(2)}) async-start(bf16[1,32,2,2048]{3,2,0,1:T(2,128)(2,1)} %copy.31), calls=%async_computation.1 | async-start | bytes 524288 | tf_op jit(solution)/shard_map/while/body/eval_jaxpr/all_to_all | solution.py:58
  753.4 12.8 %all-to-all-start = ((bf16[32,1,2,2048]{3,2,1,0:T(2,128)(2,1)}), bf16[32,1,2,2048]{3,2,1,0:T(2,128)(2,1)S(1)}, u32[]{:S(2)}, u32[]{:S(2)}) async-start(bf16[32,1,2,2048]{3,2,1,0:T(2,128)(2,1)} %bitcast.85), calls=%async_computation | async-start | bytes 524288 | tf_op jit(solution)/shard_map/while/body/eval_jaxpr/all_to_all | solution.py:53
  771.4 12.8 %all-to-all-start.1 = ((bf16[1,32,2,2048]{3,2,0,1:T(2,128)(2,1)}), bf16[1,32,2,2048]{3,2,0,1:T(2,128)(2,1)S(1)}, u32[]{:S(2)}, u32[]{:S(2)}) async-start(bf16[1,32,2,2048]{3,2,0,1:T(2,128)(2,1)} %copy.31), calls=%async_computation.1 | async-start | bytes 524288 | tf_op jit(solution)/shard_map/while/body/eval_jaxpr/all_to_all | solution.py:58
  797.8 12.8 %all-to-all-start = ((bf16[32,1,2,2048]{3,2,1,0:T(2,128)(2,1)}), bf16[32,1,2,2048]{3,2,1,0:T(2,128)(2,1)S(1)}, u32[]{:S(2)}, u32[]{:S(2)}) async-start(bf16[32,1,2,2048]{3,2,1,0:T(2,128)(2,1)} %bitcast.85), calls=%async_computation | async-start | bytes 524288 | tf_op jit(solution)/shard_map/while/body/eval_jaxpr/all_to_all | solution.py:53
  815.8 12.8 %all-to-all-start.1 = ((bf16[1,32,2,2048]{3,2,0,1:T(2,128)(2,1)}), bf16[1,32,2,2048]{3,2,0,1:T(2,128)(2,1)S(1)}, u32[]{:S(2)}, u32[]{:S(2)}) async-start(bf16[1,32,2,2048]{3,2,0,1:T(2,128)(2,1)} %copy.31), calls=%async_computation.1 | async-start | bytes 524288 | tf_op jit(solution)/shard_map/while/body/eval_jaxpr/all_to_all | solution.py:58
  842.2 12.8 %all-to-all-start = ((bf16[32,1,2,2048]{3,2,1,0:T(2,128)(2,1)}), bf16[32,1,2,2048]{3,2,1,0:T(2,128)(2,1)S(1)}, u32[]{:S(2)}, u32[]{:S(2)}) async-start(bf16[32,1,2,2048]{3,2,1,0:T(2,128)(2,1)} %bitcast.85), calls=%async_computation | async-start | bytes 524288 | tf_op jit(solution)/shard_map/while/body/eval_jaxpr/all_to_all | solution.py:53
  860.3 12.8 %all-to-all-start.1 = ((bf16[1,32,2,2048]{3,2,0,1:T(2,128)(2,1)}), bf16[1,32,2,2048]{3,2,0,1:T(2,128)(2,1)S(1)}, u32[]{:S(2)}, u32[]{:S(2)}) async-start(bf16[1,32,2,2048]{3,2,0,1:T(2,128)(2,1)} %copy.31), calls=%async_computation.1 | async-start | bytes 524288 | tf_op jit(solution)/shard_map/while/body/eval_jaxpr/all_to_all | solution.py:58
  886.7 12.8 %all-to-all-start = ((bf16[32,1,2,2048]{3,2,1,0:T(2,128)(2,1)}), bf16[32,1,2,2048]{3,2,1,0:T(2,128)(2,1)S(1)}, u32[]{:S(2)}, u32[]{:S(2)}) async-start(bf16[32,1,2,2048]{3,2,1,0:T(2,128)(2,1)} %bitcast.85), calls=%async_computation | async-start | bytes 524288 | tf_op jit(solution)/shard_map/while/body/eval_jaxpr/all_to_all | solution.py:53
  904.7 12.8 %all-to-all-start.1 = ((bf16[1,32,2,2048]{3,2,0,1:T(2,128)(2,1)}), bf16[1,32,2,2048]{3,2,0,1:T(2,128)(2,1)S(1)}, u32[]{:S(2)}, u32[]{:S(2)}) async-start(bf16[1,32,2,2048]{3,2,0,1:T(2,128)(2,1)} %copy.31), calls=%async_computation.1 | async-start | bytes 524288 | tf_op jit(solution)/shard_map/while/body/eval_jaxpr/all_to_all | solution.py:58
  931.1 12.8 %all-to-all-start = ((bf16[32,1,2,2048]{3,2,1,0:T(2,128)(2,1)}), bf16[32,1,2,2048]{3,2,1,0:T(2,128)(2,1)S(1)}, u32[]{:S(2)}, u32[]{:S(2)}) async-start(bf16[32,1,2,2048]{3,2,1,0:T(2,128)(2,1)} %bitcast.85), calls=%async_computation | async-start | bytes 524288 | tf_op jit(solution)/shard_map/while/body/eval_jaxpr/all_to_all | solution.py:53
  949.1 12.8 %all-to-all-start.1 = ((bf16[1,32,2,2048]{3,2,0,1:T(2,128)(2,1)}), bf16[1,32,2,2048]{3,2,0,1:T(2,128)(2,1)S(1)}, u32[]{:S(2)}, u32[]{:S(2)}) async-start(bf16[1,32,2,2048]{3,2,0,1:T(2,128)(2,1)} %copy.31), calls=%async_computation.1 | async-start | bytes 524288 | tf_op jit(solution)/shard_map/while/body/eval_jaxpr/all_to_all | solution.py:58
  975.5 12.8 %all-to-all-start = ((bf16[32,1,2,2048]{3,2,1,0:T(2,128)(2,1)}), bf16[32,1,2,2048]{3,2,1,0:T(2,128)(2,1)S(1)}, u32[]{:S(2)}, u32[]{:S(2)}) async-start(bf16[32,1,2,2048]{3,2,1,0:T(2,128)(2,1)} %bitcast.85), calls=%async_computation | async-start | bytes 524288 | tf_op jit(solution)/shard_map/while/body/eval_jaxpr/all_to_all | solution.py:53
  993.5 12.8 %all-to-all-start.1 = ((bf16[1,32,2,2048]{3,2,0,1:T(2,128)(2,1)}), bf16[1,32,2,2048]{3,2,0,1:T(2,128)(2,1)S(1)}, u32[]{:S(2)}, u32[]{:S(2)}) async-start(bf16[1,32,2,2048]{3,2,0,1:T(2,128)(2,1)} %copy.31), calls=%async_computation.1 | async-start | bytes 524288 | tf_op jit(solution)/shard_map/while/body/eval_jaxpr/all_to_all | solution.py:58
  1019.9 12.8 %all-to-all-start = ((bf16[32,1,2,2048]{3,2,1,0:T(2,128)(2,1)}), bf16[32,1,2,2048]{3,2,1,0:T(2,128)(2,1)S(1)}, u32[]{:S(2)}, u32[]{:S(2)}) async-start(bf16[32,1,2,2048]{3,2,1,0:T(2,128)(2,1)} %bitcast.85), calls=%async_computation | async-start | bytes 524288 | tf_op jit(solution)/shard_map/while/body/eval_jaxpr/all_to_all | solution.py:53
  1038.0 12.8 %all-to-all-start.1 = ((bf16[1,32,2,2048]{3,2,0,1:T(2,128)(2,1)}), bf16[1,32,2,2048]{3,2,0,1:T(2,128)(2,1)S(1)}, u32[]{:S(2)}, u32[]{:S(2)}) async-start(bf16[1,32,2,2048]{3,2,0,1:T(2,128)(2,1)} %copy.31), calls=%async_computation.1 | async-start | bytes 524288 | tf_op jit(solution)/shard_map/while/body/eval_jaxpr/all_to_all | solution.py:58
  (67 other events, 890.3 us)
where the time goes:
time: 1070 us; the launch traced here: 1060 us
  waiting for transfers between devices  469 us (44%)
  starting transfers between devices  226 us (21%)
  matrix products  138 us (13%)
  other arithmetic  102 us (10%)
  local copies, waits for them, and re-layouts  89 us (8%)
  blocking collectives  33.5 us (3%)
    all_to_all x23, waiting for transfers between devices, moe_layer(): lax.all_to_all(results, 'expert', split_axis=1, concat_axis=0, tiled=True)  185 us
    all_to_all x23, waiting for transfers between devices, moe_layer(): lax.all_to_all(sending, 'expert', split_axis=0, concat_axis=1, tiled=True)  168 us
    ppermute x23, waiting for transfers between devices, passed_along(): return lax.ppermute(value, axis, pairs)  116 us
    all_to_all x23, starting transfers between devices, moe_layer(): lax.all_to_all(sending, 'expert', split_axis=0, concat_axis=1, tiled=True)  92.5 us
    all_to_all x23, starting transfers between devices, moe_layer(): lax.all_to_all(results, 'expert', split_axis=1, concat_axis=0, tiled=True)  88.9 us
    ppermute x23, starting transfers between devices, passed_along(): return lax.ppermute(value, axis, pairs)  44.7 us
    convert_element_type x23, local copies, waits for them, and re-layouts, expert_block(): jnp.einsum('escf,efd->escd', active, w_down, preferred_element_type=jnp.f...  44.2 us
    dot_general x23, matrix products, expert_block(): jnp.einsum('escd,edf->escf', routed, w_gate, preferred_element_type=jnp.f...  40.5 us
  transfers between devices with their start and end apart: 69, of which 69 were waited for; matrix products, arithmetic and copies ran while one was open for 5% of the time, Pallas kernels for 0%

commit v1 on v0

--- a/solution.py
+++ b/solution.py
@@ -68,7 +68,24 @@
 def local(tokens, norm_gain, gate_weight, up_weight, down_weight, expert_ids, gate_probs):
     section_index = lax.axis_index("section")
     section_count = lax.axis_size("section")
-    full_tokens = lax.all_gather(tokens, "section", axis=2, tiled=True)
+    length_2, index, span = (lax.axis_size("section"), lax.axis_index("section"), tokens.shape[2])
+    ahead = [(i_2, (i_2 + 1) % length_2) for i_2 in range(length_2)]
+    backward = [(i_2, (i_2 - 1) % length_2) for i_2 in range(length_2)]
+    whole = jnp.zeros((*tokens.shape[:2], length_2 * span, *tokens.shape[2 + 1 :]), tokens.dtype)
+    whole = lax.dynamic_update_slice_in_dim(whole, tokens, index * span, axis=2)
+    from_left = from_right = tokens
+    middle = length_2 // 2
+    for step in range(1, middle + 1):
+        from_left = lax.ppermute(from_left, "section", ahead)
+        whole = lax.dynamic_update_slice_in_dim(
+            whole, from_left, (index - step) % length_2 * span, axis=2
+        )
+        if step < length_2 - middle:
+            from_right = lax.ppermute(from_right, "section", backward)
+            whole = lax.dynamic_update_slice_in_dim(
+                whole, from_right, (index + step) % length_2 * span, axis=2
+            )
+    full_tokens = whole
     micro_count, row_count, columns = full_tokens.shape
     turn_count = section_count + micro_count - 1
     norm_scale = norm_gain[0]

time: 1070 us -> 1090 us (1.019)
  the two profiles are of different devices: /device:TPU:128 before, /device:TPU:384 now
where the time goes in v1:
time: 1090 us; the launch traced here: 1070 us
  waiting for transfers between devices  474 us (43%)
  starting transfers between devices  277 us (25%)
  matrix products  119 us (11%)
  other arithmetic  102 us (9%)
  local copies, waits for them, and re-layouts  100 us (9%)
    all_to_all x23, waiting for transfers between devices, moe_layer(): lax.all_to_all(results, 'expert', split_axis=1, concat_axis=0, tiled=True)  185 us
    all_to_all x23, waiting for transfers between devices, moe_layer(): lax.all_to_all(sending, 'expert', split_axis=0, concat_axis=1, tiled=True)  168 us
    ppermute x23, waiting for transfers between devices, passed_along(): return lax.ppermute(value, axis, pairs)  117 us
    all_to_all x23, starting transfers between devices, moe_layer(): lax.all_to_all(sending, 'expert', split_axis=0, concat_axis=1, tiled=True)  92.4 us
    all_to_all x23, starting transfers between devices, moe_layer(): lax.all_to_all(results, 'expert', split_axis=1, concat_axis=0, tiled=True)  89 us
    convert_element_type x23, local copies, waits for them, and re-layouts, expert_block(): jnp.einsum('escf,efd->escd', active, w_down, preferred_element_type=jnp.f...  44.5 us
    ppermute x23, starting transfers between devices, passed_along(): return lax.ppermute(value, axis, pairs)  43.9 us
    dot_general x23, matrix products, expert_block(): jnp.einsum('escd,edf->escf', routed, w_gate, preferred_element_type=jnp.f...  40.6 us
  transfers between devices with their start and end apart: 84, of which 70 were waited for; matrix products, arithmetic and copies ran while one was open for 6% of the time, Pallas kernels for 0%

profile of v1, /device:TPU:384, one launch (start us, length us, event | category | flops | bytes accessed | tf_op | source)
XLA Modules:
  0.0 1073.4 jit_solution(15136219707974554994)
XLA Ops:
  67.1 1006.2 %while.17 = (s32[]{:T(128)}, bf16[8,2048]{1,0:T(8,128)(2,1)S(1)}, bf16[8,8,2048]{2,1,0:T(8,128)(2,1)}, pred[]{:T(512)}, s32[]{:T(128)}, /*index=5*/bf16[8,8,2048...) while((s32[]{:T(128)}, bf16[8,2048]{1,0:T(8,128)(2,1)S(1)}, ...), condition=%wide.region_7.8_spmd, body=%wide.region_0.7_spmd.sunk | while | flops 317443392 | bytes 16109876 | solution.py:119
  71.2 7.3 all-to-all-start
  80.1 7.3 all-to-all-done
  97.4 8.0 all-to-all-done.1
  123.7 7.3 all-to-all-done
  141.0 8.0 all-to-all-done.1
  167.3 7.3 all-to-all-done
  184.6 8.0 all-to-all-done.1
  210.9 7.3 all-to-all-done
  228.2 8.0 all-to-all-done.1
  254.5 7.3 all-to-all-done
  271.8 8.0 all-to-all-done.1
  298.1 7.3 all-to-all-done
  315.4 8.0 all-to-all-done.1
  341.7 7.3 all-to-all-done
  359.0 8.0 all-to-all-done.1
  385.3 7.3 all-to-all-done
  402.6 8.0 all-to-all-done.1
  428.9 7.3 all-to-all-done
  446.2 8.0 all-to-all-done.1
  472.5 7.3 all-to-all-done
  489.8 8.0 all-to-all-done.1
  516.1 7.3 all-to-all-done
  533.4 8.0 all-to-all-done.1
  559.7 7.3 all-to-all-done
  577.0 8.0 all-to-all-done.1
  603.3 7.3 all-to-all-done
  620.6 8.0 all-to-all-done.1
  646.9 7.3 all-to-all-done
  664.2 8.0 all-to-all-done.1
  690.5 7.3 all-to-all-done
  707.8 8.0 all-to-all-done.1
  734.1 7.3 all-to-all-done
  751.4 8.0 all-to-all-done.1
  777.7 7.3 all-to-all-done
  795.0 8.0 all-to-all-done.1
  821.3 7.3 all-to-all-done
  838.6 8.0 all-to-all-done.1
  864.9 7.3 all-to-all-done
  882.2 8.0 all-to-all-done.1
  908.5 7.3 all-to-all-done
  925.8 8.0 all-to-all-done.1
  952.1 7.3 all-to-all-done
  969.4 8.0 all-to-all-done.1
  995.7 7.3 all-to-all-done
  1013.0 8.0 all-to-all-done.1
  1039.3 7.3 all-to-all-done
  1056.6 8.0 all-to-all-done.1
  (696 shorter events, 710.8 us)
Async XLA Ops:
  0.0 9.2 collective-permute-start.1
  52.6 8.9 collective-permute-start.14
  71.2 16.2 %all-to-all-start = ((bf16[32,1,2,2048]{3,2,1,0:T(2,128)(2,1)}), bf16[32,1,2,2048]{3,2,1,0:T(2,128)(2,1)S(1)}, u32[]{:S(2)}, u32[]{:S(2)}) async-start(bf16[32,1,2,2048]{3,2,1,0:T(2,128)(2,1)} %bitcast.85), calls=%async_computation | async-start | bytes 524288 | tf_op jit(solution)/shard_map/while/body/eval_jaxpr/all_to_all | solution.py:53
  92.7 12.8 %all-to-all-start.1 = ((bf16[1,32,2,2048]{3,2,0,1:T(2,128)(2,1)}), bf16[1,32,2,2048]{3,2,0,1:T(2,128)(2,1)S(1)}, u32[]{:S(2)}, u32[]{:S(2)}) async-start(bf16[1,32,2,2048]{3,2,0,1:T(2,128)(2,1)} %copy.31), calls=%async_computation.1 | async-start | bytes 524288 | tf_op jit(solution)/shard_map/while/body/eval_jaxpr/all_to_all | solution.py:58
  118.3 12.8 %all-to-all-start = ((bf16[32,1,2,2048]{3,2,1,0:T(2,128)(2,1)}), bf16[32,1,2,2048]{3,2,1,0:T(2,128)(2,1)S(1)}, u32[]{:S(2)}, u32[]{:S(2)}) async-start(bf16[32,1,2,2048]{3,2,1,0:T(2,128)(2,1)} %bitcast.85), calls=%async_computation | async-start | bytes 524288 | tf_op jit(solution)/shard_map/while/body/eval_jaxpr/all_to_all | solution.py:53
  136.3 12.8 %all-to-all-start.1 = ((bf16[1,32,2,2048]{3,2,0,1:T(2,128)(2,1)}), bf16[1,32,2,2048]{3,2,0,1:T(2,128)(2,1)S(1)}, u32[]{:S(2)}, u32[]{:S(2)}) async-start(bf16[1,32,2,2048]{3,2,0,1:T(2,128)(2,1)} %copy.31), calls=%async_computation.1 | async-start | bytes 524288 | tf_op jit(solution)/shard_map/while/body/eval_jaxpr/all_to_all | solution.py:58
  161.9 12.8 %all-to-all-start = ((bf16[32,1,2,2048]{3,2,1,0:T(2,128)(2,1)}), bf16[32,1,2,2048]{3,2,1,0:T(2,128)(2,1)S(1)}, u32[]{:S(2)}, u32[]{:S(2)}) async-start(bf16[32,1,2,2048]{3,2,1,0:T(2,128)(2,1)} %bitcast.85), calls=%async_computation | async-start | bytes 524288 | tf_op jit(solution)/shard_map/while/body/eval_jaxpr/all_to_all | solution.py:53
  179.9 12.8 %all-to-all-start.1 = ((bf16[1,32,2,2048]{3,2,0,1:T(2,128)(2,1)}), bf16[1,32,2,2048]{3,2,0,1:T(2,128)(2,1)S(1)}, u32[]{:S(2)}, u32[]{:S(2)}) async-start(bf16[1,32,2,2048]{3,2,0,1:T(2,128)(2,1)} %copy.31), calls=%async_computation.1 | async-start | bytes 524288 | tf_op jit(solution)/shard_map/while/body/eval_jaxpr/all_to_all | solution.py:58
  205.5 12.8 %all-to-all-start = ((bf16[32,1,2,2048]{3,2,1,0:T(2,128)(2,1)}), bf16[32,1,2,2048]{3,2,1,0:T(2,128)(2,1)S(1)}, u32[]{:S(2)}, u32[]{:S(2)}) async-start(bf16[32,1,2,2048]{3,2,1,0:T(2,128)(2,1)} %bitcast.85), calls=%async_computation | async-start | bytes 524288 | tf_op jit(solution)/shard_map/while/body/eval_jaxpr/all_to_all | solution.py:53
  223.5 12.8 %all-to-all-start.1 = ((bf16[1,32,2,2048]{3,2,0,1:T(2,128)(2,1)}), bf16[1,32,2,2048]{3,2,0,1:T(2,128)(2,1)S(1)}, u32[]{:S(2)}, u32[]{:S(2)}) async-start(bf16[1,32,2,2048]{3,2,0,1:T(2,128)(2,1)} %copy.31), calls=%async_computation.1 | async-start | bytes 524288 | tf_op jit(solution)/shard_map/while/body/eval_jaxpr/all_to_all | solution.py:58
  249.1 12.8 %all-to-all-start = ((bf16[32,1,2,2048]{3,2,1,0:T(2,128)(2,1)}), bf16[32,1,2,2048]{3,2,1,0:T(2,128)(2,1)S(1)}, u32[]{:S(2)}, u32[]{:S(2)}) async-start(bf16[32,1,2,2048]{3,2,1,0:T(2,128)(2,1)} %bitcast.85), calls=%async_computation | async-start | bytes 524288 | tf_op jit(solution)/shard_map/while/body/eval_jaxpr/all_to_all | solution.py:53
  267.1 12.8 %all-to-all-start.1 = ((bf16[1,32,2,2048]{3,2,0,1:T(2,128)(2,1)}), bf16[1,32,2,2048]{3,2,0,1:T(2,128)(2,1)S(1)}, u32[]{:S(2)}, u32[]{:S(2)}) async-start(bf16[1,32,2,2048]{3,2,0,1:T(2,128)(2,1)} %copy.31), calls=%async_computation.1 | async-start | bytes 524288 | tf_op jit(solution)/shard_map/while/body/eval_jaxpr/all_to_all | solution.py:58
  292.7 12.8 %all-to-all-start = ((bf16[32,1,2,2048]{3,2,1,0:T(2,128)(2,1)}), bf16[32,1,2,2048]{3,2,1,0:T(2,128)(2,1)S(1)}, u32[]{:S(2)}, u32[]{:S(2)}) async-start(bf16[32,1,2,2048]{3,2,1,0:T(2,128)(2,1)} %bitcast.85), calls=%async_computation | async-start | bytes 524288 | tf_op jit(solution)/shard_map/while/body/eval_jaxpr/all_to_all | solution.py:53
  310.7 12.8 %all-to-all-start.1 = ((bf16[1,32,2,2048]{3,2,0,1:T(2,128)(2,1)}), bf16[1,32,2,2048]{3,2,0,1:T(2,128)(2,1)S(1)}, u32[]{:S(2)}, u32[]{:S(2)}) async-start(bf16[1,32,2,2048]{3,2,0,1:T(2,128)(2,1)} %copy.31), calls=%async_computation.1 | async-start | bytes 524288 | tf_op jit(solution)/shard_map/while/body/eval_jaxpr/all_to_all | solution.py:58
  336.3 12.8 %all-to-all-start = ((bf16[32,1,2,2048]{3,2,1,0:T(2,128)(2,1)}), bf16[32,1,2,2048]{3,2,1,0:T(2,128)(2,1)S(1)}, u32[]{:S(2)}, u32[]{:S(2)}) async-start(bf16[32,1,2,2048]{3,2,1,0:T(2,128)(2,1)} %bitcast.85), calls=%async_computation | async-start | bytes 524288 | tf_op jit(solution)/shard_map/while/body/eval_jaxpr/all_to_all | solution.py:53
  354.3 12.8 %all-to-all-start.1 = ((bf16[1,32,2,2048]{3,2,0,1:T(2,128)(2,1)}), bf16[1,32,2,2048]{3,2,0,1:T(2,128)(2,1)S(1)}, u32[]{:S(2)}, u32[]{:S(2)}) async-start(bf16[1,32,2,2048]{3,2,0,1:T(2,128)(2,1)} %copy.31), calls=%async_computation.1 | async-start | bytes 524288 | tf_op jit(solution)/shard_map/while/body/eval_jaxpr/all_to_all | solution.py:58
  379.9 12.8 %all-to-all-start = ((bf16[32,1,2,2048]{3,2,1,0:T(2,128)(2,1)}), bf16[32,1,2,2048]{3,2,1,0:T(2,128)(2,1)S(1)}, u32[]{:S(2)}, u32[]{:S(2)}) async-start(bf16[32,1,2,2048]{3,2,1,0:T(2,128)(2,1)} %bitcast.85), calls=%async_computation | async-start | bytes 524288 | tf_op jit(solution)/shard_map/while/body/eval_jaxpr/all_to_all | solution.py:53
  397.9 12.8 %all-to-all-start.1 = ((bf16[1,32,2,2048]{3,2,0,1:T(2,128)(2,1)}), bf16[1,32,2,2048]{3,2,0,1:T(2,128)(2,1)S(1)}, u32[]{:S(2)}, u32[]{:S(2)}) async-start(bf16[1,32,2,2048]{3,2,0,1:T(2,128)(2,1)} %copy.31), calls=%async_computation.1 | async-start | bytes 524288 | tf_op jit(solution)/shard_map/while/body/eval_jaxpr/all_to_all | solution.py:58
  423.5 12.8 %all-to-all-start = ((bf16[32,1,2,2048]{3,2,1,0:T(2,128)(2,1)}), bf16[32,1,2,2048]{3,2,1,0:T(2,128)(2,1)S(1)}, u32[]{:S(2)}, u32[]{:S(2)}) async-start(bf16[32,1,2,2048]{3,2,1,0:T(2,128)(2,1)} %bitcast.85), calls=%async_computation | async-start | bytes 524288 | tf_op jit(solution)/shard_map/while/body/eval_jaxpr/all_to_all | solution.py:53
  441.5 12.8 %all-to-all-start.1 = ((bf16[1,32,2,2048]{3,2,0,1:T(2,128)(2,1)}), bf16[1,32,2,2048]{3,2,0,1:T(2,128)(2,1)S(1)}, u32[]{:S(2)}, u32[]{:S(2)}) async-start(bf16[1,32,2,2048]{3,2,0,1:T(2,128)(2,1)} %copy.31), calls=%async_computation.1 | async-start | bytes 524288 | tf_op jit(solution)/shard_map/while/body/eval_jaxpr/all_to_all | solution.py:58
  467.1 12.8 %all-to-all-start = ((bf16[32,1,2,2048]{3,2,1,0:T(2,128)(2,1)}), bf16[32,1,2,2048]{3,2,1,0:T(2,128)(2,1)S(1)}, u32[]{:S(2)}, u32[]{:S(2)}) async-start(bf16[32,1,2,2048]{3,2,1,0:T(2,128)(2,1)} %bitcast.85), calls=%async_computation | async-start | bytes 524288 | tf_op jit(solution)/shard_map/while/body/eval_jaxpr/all_to_all | solution.py:53
  485.1 12.8 %all-to-all-start.1 = ((bf16[1,32,2,2048]{3,2,0,1:T(2,128)(2,1)}), bf16[1,32,2,2048]{3,2,0,1:T(2,128)(2,1)S(1)}, u32[]{:S(2)}, u32[]{:S(2)}) async-start(bf16[1,32,2,2048]{3,2,0,1:T(2,128)(2,1)} %copy.31), calls=%async_computation.1 | async-start | bytes 524288 | tf_op jit(solution)/shard_map/while/body/eval_jaxpr/all_to_all | solution.py:58
  510.7 12.8 %all-to-all-start = ((bf16[32,1,2,2048]{3,2,1,0:T(2,128)(2,1)}), bf16[32,1,2,2048]{3,2,1,0:T(2,128)(2,1)S(1)}, u32[]{:S(2)}, u32[]{:S(2)}) async-start(bf16[32,1,2,2048]{3,2,1,0:T(2,128)(2,1)} %bitcast.85), calls=%async_computation | async-start | bytes 524288 | tf_op jit(solution)/shard_map/while/body/eval_jaxpr/all_to_all | solution.py:53
  528.7 12.8 %all-to-all-start.1 = ((bf16[1,32,2,2048]{3,2,0,1:T(2,128)(2,1)}), bf16[1,32,2,2048]{3,2,0,1:T(2,128)(2,1)S(1)}, u32[]{:S(2)}, u32[]{:S(2)}) async-start(bf16[1,32,2,2048]{3,2,0,1:T(2,128)(2,1)} %copy.31), calls=%async_computation.1 | async-start | bytes 524288 | tf_op jit(solution)/shard_map/while/body/eval_jaxpr/all_to_all | solution.py:58
  554.3 12.8 %all-to-all-start = ((bf16[32,1,2,2048]{3,2,1,0:T(2,128)(2,1)}), bf16[32,1,2,2048]{3,2,1,0:T(2,128)(2,1)S(1)}, u32[]{:S(2)}, u32[]{:S(2)}) async-start(bf16[32,1,2,2048]{3,2,1,0:T(2,128)(2,1)} %bitcast.85), calls=%async_computation | async-start | bytes 524288 | tf_op jit(solution)/shard_map/while/body/eval_jaxpr/all_to_all | solution.py:53
  572.3 12.8 %all-to-all-start.1 = ((bf16[1,32,2,2048]{3,2,0,1:T(2,128)(2,1)}), bf16[1,32,2,2048]{3,2,0,1:T(2,128)(2,1)S(1)}, u32[]{:S(2)}, u32[]{:S(2)}) async-start(bf16[1,32,2,2048]{3,2,0,1:T(2,128)(2,1)} %copy.31), calls=%async_computation.1 | async-start | bytes 524288 | tf_op jit(solution)/shard_map/while/body/eval_jaxpr/all_to_all | solution.py:58
  597.9 12.8 %all-to-all-start = ((bf16[32,1,2,2048]{3,2,1,0:T(2,128)(2,1)}), bf16[32,1,2,2048]{3,2,1,0:T(2,128)(2,1)S(1)}, u32[]{:S(2)}, u32[]{:S(2)}) async-start(bf16[32,1,2,2048]{3,2,1,0:T(2,128)(2,1)} %bitcast.85), calls=%async_computation | async-start | bytes 524288 | tf_op jit(solution)/shard_map/while/body/eval_jaxpr/all_to_all | solution.py:53
  615.9 12.8 %all-to-all-start.1 = ((bf16[1,32,2,2048]{3,2,0,1:T(2,128)(2,1)}), bf16[1,32,2,2048]{3,2,0,1:T(2,128)(2,1)S(1)}, u32[]{:S(2)}, u32[]{:S(2)}) async-start(bf16[1,32,2,2048]{3,2,0,1:T(2,128)(2,1)} %copy.31), calls=%async_computation.1 | async-start | bytes 524288 | tf_op jit(solution)/shard_map/while/body/eval_jaxpr/all_to_all | solution.py:58
  641.5 12.8 %all-to-all-start = ((bf16[32,1,2,2048]{3,2,1,0:T(2,128)(2,1)}), bf16[32,1,2,2048]{3,2,1,0:T(2,128)(2,1)S(1)}, u32[]{:S(2)}, u32[]{:S(2)}) async-start(bf16[32,1,2,2048]{3,2,1,0:T(2,128)(2,1)} %bitcast.85), calls=%async_computation | async-start | bytes 524288 | tf_op jit(solution)/shard_map/while/body/eval_jaxpr/all_to_all | solution.py:53
  659.5 12.8 %all-to-all-start.1 = ((bf16[1,32,2,2048]{3,2,0,1:T(2,128)(2,1)}), bf16[1,32,2,2048]{3,2,0,1:T(2,128)(2,1)S(1)}, u32[]{:S(2)}, u32[]{:S(2)}) async-start(bf16[1,32,2,2048]{3,2,0,1:T(2,128)(2,1)} %copy.31), calls=%async_computation.1 | async-start | bytes 524288 | tf_op jit(solution)/shard_map/while/body/eval_jaxpr/all_to_all | solution.py:58
  685.1 12.8 %all-to-all-start = ((bf16[32,1,2,2048]{3,2,1,0:T(2,128)(2,1)}), bf16[32,1,2,2048]{3,2,1,0:T(2,128)(2,1)S(1)}, u32[]{:S(2)}, u32[]{:S(2)}) async-start(bf16[32,1,2,2048]{3,2,1,0:T(2,128)(2,1)} %bitcast.85), calls=%async_computation | async-start | bytes 524288 | tf_op jit(solution)/shard_map/while/body/eval_jaxpr/all_to_all | solution.py:53
  703.1 12.8 %all-to-all-start.1 = ((bf16[1,32,2,2048]{3,2,0,1:T(2,128)(2,1)}), bf16[1,32,2,2048]{3,2,0,1:T(2,128)(2,1)S(1)}, u32[]{:S(2)}, u32[]{:S(2)}) async-start(bf16[1,32,2,2048]{3,2,0,1:T(2,128)(2,1)} %copy.31), calls=%async_computation.1 | async-start | bytes 524288 | tf_op jit(solution)/shard_map/while/body/eval_jaxpr/all_to_all | solution.py:58
  728.7 12.8 %all-to-all-start = ((bf16[32,1,2,2048]{3,2,1,0:T(2,128)(2,1)}), bf16[32,1,2,2048]{3,2,1,0:T(2,128)(2,1)S(1)}, u32[]{:S(2)}, u32[]{:S(2)}) async-start(bf16[32,1,2,2048]{3,2,1,0:T(2,128)(2,1)} %bitcast.85), calls=%async_computation | async-start | bytes 524288 | tf_op jit(solution)/shard_map/while/body/eval_jaxpr/all_to_all | solution.py:53
  746.7 12.8 %all-to-all-start.1 = ((bf16[1,32,2,2048]{3,2,0,1:T(2,128)(2,1)}), bf16[1,32,2,2048]{3,2,0,1:T(2,128)(2,1)S(1)}, u32[]{:S(2)}, u32[]{:S(2)}) async-start(bf16[1,32,2,2048]{3,2,0,1:T(2,128)(2,1)} %copy.31), calls=%async_computation.1 | async-start | bytes 524288 | tf_op jit(solution)/shard_map/while/body/eval_jaxpr/all_to_all | solution.py:58
  772.3 12.8 %all-to-all-start = ((bf16[32,1,2,2048]{3,2,1,0:T(2,128)(2,1)}), bf16[32,1,2,2048]{3,2,1,0:T(2,128)(2,1)S(1)}, u32[]{:S(2)}, u32[]{:S(2)}) async-start(bf16[32,1,2,2048]{3,2,1,0:T(2,128)(2,1)} %bitcast.85), calls=%async_computation | async-start | bytes 524288 | tf_op jit(solution)/shard_map/while/body/eval_jaxpr/all_to_all | solution.py:53
  790.3 12.8 %all-to-all-start.1 = ((bf16[1,32,2,2048]{3,2,0,1:T(2,128)(2,1)}), bf16[1,32,2,2048]{3,2,0,1:T(2,128)(2,1)S(1)}, u32[]{:S(2)}, u32[]{:S(2)}) async-start(bf16[1,32,2,2048]{3,2,0,1:T(2,128)(2,1)} %copy.31), calls=%async_computation.1 | async-start | bytes 524288 | tf_op jit(solution)/shard_map/while/body/eval_jaxpr/all_to_all | solution.py:58
  815.9 12.8 %all-to-all-start = ((bf16[32,1,2,2048]{3,2,1,0:T(2,128)(2,1)}), bf16[32,1,2,2048]{3,2,1,0:T(2,128)(2,1)S(1)}, u32[]{:S(2)}, u32[]{:S(2)}) async-start(bf16[32,1,2,2048]{3,2,1,0:T(2,128)(2,1)} %bitcast.85), calls=%async_computation | async-start | bytes 524288 | tf_op jit(solution)/shard_map/while/body/eval_jaxpr/all_to_all | solution.py:53
  833.9 12.8 %all-to-all-start.1 = ((bf16[1,32,2,2048]{3,2,0,1:T(2,128)(2,1)}), bf16[1,32,2,2048]{3,2,0,1:T(2,128)(2,1)S(1)}, u32[]{:S(2)}, u32[]{:S(2)}) async-start(bf16[1,32,2,2048]{3,2,0,1:T(2,128)(2,1)} %copy.31), calls=%async_computation.1 | async-start | bytes 524288 | tf_op jit(solution)/shard_map/while/body/eval_jaxpr/all_to_all | solution.py:58
  859.5 12.8 %all-to-all-start = ((bf16[32,1,2,2048]{3,2,1,0:T(2,128)(2,1)}), bf16[32,1,2,2048]{3,2,1,0:T(2,128)(2,1)S(1)}, u32[]{:S(2)}, u32[]{:S(2)}) async-start(bf16[32,1,2,2048]{3,2,1,0:T(2,128)(2,1)} %bitcast.85), calls=%async_computation | async-start | bytes 524288 | tf_op jit(solution)/shard_map/while/body/eval_jaxpr/all_to_all | solution.py:53
  877.5 12.8 %all-to-all-start.1 = ((bf16[1,32,2,2048]{3,2,0,1:T(2,128)(2,1)}), bf16[1,32,2,2048]{3,2,0,1:T(2,128)(2,1)S(1)}, u32[]{:S(2)}, u32[]{:S(2)}) async-start(bf16[1,32,2,2048]{3,2,0,1:T(2,128)(2,1)} %copy.31), calls=%async_computation.1 | async-start | bytes 524288 | tf_op jit(solution)/shard_map/while/body/eval_jaxpr/all_to_all | solution.py:58
  903.1 12.8 %all-to-all-start = ((bf16[32,1,2,2048]{3,2,1,0:T(2,128)(2,1)}), bf16[32,1,2,2048]{3,2,1,0:T(2,128)(2,1)S(1)}, u32[]{:S(2)}, u32[]{:S(2)}) async-start(bf16[32,1,2,2048]{3,2,1,0:T(2,128)(2,1)} %bitcast.85), calls=%async_computation | async-start | bytes 524288 | tf_op jit(solution)/shard_map/while/body/eval_jaxpr/all_to_all | solution.py:53
  921.1 12.8 %all-to-all-start.1 = ((bf16[1,32,2,2048]{3,2,0,1:T(2,128)(2,1)}), bf16[1,32,2,2048]{3,2,0,1:T(2,128)(2,1)S(1)}, u32[]{:S(2)}, u32[]{:S(2)}) async-start(bf16[1,32,2,2048]{3,2,0,1:T(2,128)(2,1)} %copy.31), calls=%async_computation.1 | async-start | bytes 524288 | tf_op jit(solution)/shard_map/while/body/eval_jaxpr/all_to_all | solution.py:58
  946.7 12.8 %all-to-all-start = ((bf16[32,1,2,2048]{3,2,1,0:T(2,128)(2,1)}), bf16[32,1,2,2048]{3,2,1,0:T(2,128)(2,1)S(1)}, u32[]{:S(2)}, u32[]{:S(2)}) async-start(bf16[32,1,2,2048]{3,2,1,0:T(2,128)(2,1)} %bitcast.85), calls=%async_computation | async-start | bytes 524288 | tf_op jit(solution)/shard_map/while/body/eval_jaxpr/all_to_all | solution.py:53
  964.7 12.8 %all-to-all-start.1 = ((bf16[1,32,2,2048]{3,2,0,1:T(2,128)(2,1)}), bf16[1,32,2,2048]{3,2,0,1:T(2,128)(2,1)S(1)}, u32[]{:S(2)}, u32[]{:S(2)}) async-start(bf16[1,32,2,2048]{3,2,0,1:T(2,128)(2,1)} %copy.31), calls=%async_computation.1 | async-start | bytes 524288 | tf_op jit(solution)/shard_map/while/body/eval_jaxpr/all_to_all | solution.py:58
  990.2 12.8 %all-to-all-start = ((bf16[32,1,2,2048]{3,2,1,0:T(2,128)(2,1)}), bf16[32,1,2,2048]{3,2,1,0:T(2,128)(2,1)S(1)}, u32[]{:S(2)}, u32[]{:S(2)}) async-start(bf16[32,1,2,2048]{3,2,1,0:T(2,128)(2,1)} %bitcast.85), calls=%async_computation | async-start | bytes 524288 | tf_op jit(solution)/shard_map/while/body/eval_jaxpr/all_to_all | solution.py:53
  1008.3 12.8 %all-to-all-start.1 = ((bf16[1,32,2,2048]{3,2,0,1:T(2,128)(2,1)}), bf16[1,32,2,2048]{3,2,0,1:T(2,128)(2,1)S(1)}, u32[]{:S(2)}, u32[]{:S(2)}) async-start(bf16[1,32,2,2048]{3,2,0,1:T(2,128)(2,1)} %copy.31), calls=%async_computation.1 | async-start | bytes 524288 | tf_op jit(solution)/shard_map/while/body/eval_jaxpr/all_to_all | solution.py:58
  1033.9 12.8 %all-to-all-start = ((bf16[32,1,2,2048]{3,2,1,0:T(2,128)(2,1)}), bf16[32,1,2,2048]{3,2,1,0:T(2,128)(2,1)S(1)}, u32[]{:S(2)}, u32[]{:S(2)}) async-start(bf16[32,1,2,2048]{3,2,1,0:T(2,128)(2,1)} %bitcast.85), calls=%async_computation | async-start | bytes 524288 | tf_op jit(solution)/shard_map/while/body/eval_jaxpr/all_to_all | solution.py:53
  1051.9 12.8 %all-to-all-start.1 = ((bf16[1,32,2,2048]{3,2,0,1:T(2,128)(2,1)}), bf16[1,32,2,2048]{3,2,0,1:T(2,128)(2,1)S(1)}, u32[]{:S(2)}, u32[]{:S(2)}) async-start(bf16[1,32,2,2048]{3,2,0,1:T(2,128)(2,1)} %copy.31), calls=%async_computation.1 | async-start | bytes 524288 | tf_op jit(solution)/shard_map/while/body/eval_jaxpr/all_to_all | solution.py:58
  (61 other events, 759.9 us)
